TPU v7x, 512 devices: a whole 4x8x8 slice. The times are simulated.
512 devices in a mesh: band: 8 (over y_lo, core), grid: 64 (over y_hi, x, z).
Axes of the slice: x: 4, y: 8 (y_hi: 2, y_lo: 4; y = y_hi * 4 + y_lo), z: 8, core: 2. Of those that a mesh axis runs over, the one named last changes fastest.
Arguments:
- orbitals: float32 [8, 2, 192, 192, 192], P('band', None, 'grid'), may hold values from -6 to 6
- occupations: float32 [8], P('band'), may hold values from 0.5 to 2
- ion_potential: float32 [192, 192, 192], P('grid'), may hold values from -0.6 to 0.6
- hxc_potential: float32 [192, 192, 192], P('grid'), may hold values from -0.4 to 0.4
Outputs:
- new_orbitals: float32 [8, 2, 192, 192, 192], P('band', None, 'grid')
- new_potential: float32 [192, 192, 192], P('grid')
All inputs are finite; a program needn't handle non-finite values.
Results may differ from a plain program's by a relative error of at most 0.0003.
Values sent between devices are 32-bit elements; how exact they have to be, the bound alone decides.
A program may use at most 64 MiB of HBM per device.

v0:
```python
import math
import jax
import jax.numpy as jnp
from jax import lax
from jax.sharding import PartitionSpec as P

BESSEL_ZERO = 0.8462873527504802
BESSEL_ONE = 0.36884204609417703
BESSEL_TWO = 0.07581776248
XC_FACTOR = 0.98474502


def tables(length):
    idx = jnp.arange(length, dtype=jnp.int32)
    angle = (idx[:, None] * idx[None, :] % length).astype(jnp.float32) * (2.0 * math.pi / length)
    return (jnp.cos(angle), jnp.sin(angle))


def transform(real_part, imag_part, form, inverse, length):
    cosine, sine = tables(length)
    high = lax.Precision.HIGHEST
    rc = jnp.einsum(form, real_part, cosine, precision=high)
    rs = jnp.einsum(form, real_part, sine, precision=high)
    ic = jnp.einsum(form, imag_part, cosine, precision=high)
    isn = jnp.einsum(form, imag_part, sine, precision=high)
    if inverse:
        scale = 1.0 / length
        return ((rc - isn) * scale, (ic + rs) * scale)
    return (rc + isn, ic - rs)


def along_z(real_part, imag_part, inverse):
    return transform(real_part, imag_part, "oxyn,nk->oxyk", inverse, real_part.shape[3])


def along_y(real_part, imag_part, inverse):
    return transform(real_part, imag_part, "oxnz,nk->oxkz", inverse, real_part.shape[2])


def along_x(real_part, imag_part, inverse):
    return transform(real_part, imag_part, "onyz,nk->okyz", inverse, real_part.shape[1])


def forward(real_part, imag_part):
    real_part, imag_part = along_z(real_part, imag_part, False)
    real_part, imag_part = along_y(real_part, imag_part, False)
    real_part, imag_part = (
        lax.all_to_all(real_part, "grid", split_axis=2, concat_axis=1, tiled=True),
        lax.all_to_all(imag_part, "grid", split_axis=2, concat_axis=1, tiled=True),
    )
    return along_x(real_part, imag_part, False)


def backward(real_part, imag_part):
    real_part, imag_part = along_x(real_part, imag_part, True)
    real_part, imag_part = (
        lax.all_to_all(real_part, "grid", split_axis=1, concat_axis=2, tiled=True),
        lax.all_to_all(imag_part, "grid", split_axis=1, concat_axis=2, tiled=True),
    )
    real_part, imag_part = along_y(real_part, imag_part, True)
    real_part, imag_part = along_z(real_part, imag_part, True)
    return (real_part, imag_part)


def frequency(idx, length):
    return jnp.where(idx < length // 2, idx, idx - length).astype(jnp.float32)


def squares_block(x_count, y_start, y_count, length):
    fx = frequency(jnp.arange(x_count, dtype=jnp.int32), length)
    fy = frequency(y_start + jnp.arange(y_count, dtype=jnp.int32), length)
    fz = frequency(jnp.arange(length, dtype=jnp.int32), length)
    return (fx * fx)[:, None, None] + (fy * fy)[None, :, None] + (fz * fz)[None, None, :]


def hartree_filter(squares, length):
    return jnp.where(squares > 0, length * math.sqrt(length) / 16.0 / (squares + 1.0), 0.0)


def local(orbitals, occupations, ion_potential, hxc_potential):
    length = orbitals.shape[-1]
    columns = length // lax.axis_size("grid")
    grid_pos = lax.axis_index("grid")
    squares = squares_block(length, grid_pos * columns, columns, length)
    kinetic = 2.0 * squares / (3.0 * (length / 2) ** 2) - 1.0
    potential = ion_potential + hxc_potential

    def hamilton(real_part, imag_part):
        fre, fim = forward(real_part, imag_part)
        back_re, back_im = backward(kinetic * fre, kinetic * fim)
        return (back_re + potential * real_part, back_im + potential * imag_part)

    psi_re = orbitals[:, 0]
    psi_im = orbitals[:, 1]
    first_re, first_im = hamilton(psi_re, psi_im)
    again_re, again_im = hamilton(first_re, first_im)
    second_re = 2.0 * again_re - psi_re
    second_im = 2.0 * again_im - psi_im
    fresh_re = BESSEL_ZERO * psi_re + 2.0 * BESSEL_ONE * first_im - 2.0 * BESSEL_TWO * second_re
    fresh_im = BESSEL_ZERO * psi_im - 2.0 * BESSEL_ONE * first_re - 2.0 * BESSEL_TWO * second_im
    new_orbitals = jnp.stack([fresh_re, fresh_im], axis=1)
    partial_value = jnp.sum(
        occupations[:, None, None, None] * (fresh_re * fresh_re + fresh_im * fresh_im), axis=0
    )
    density = lax.psum(partial_value, "band")
    fre, fim = forward(density[None], jnp.zeros_like(density)[None])
    kernel = hartree_filter(squares, length)
    hart_re, hart_im = backward(kernel * fre, kernel * fim)
    new_potential = hart_re[0] - XC_FACTOR * jnp.cbrt(density)
    return (new_orbitals, new_potential)


def solution(mesh):
    placed = (
        P("band", None, "grid", None, None),
        P("band"),
        P("grid", None, None),
        P("grid", None, None),
    )
    return jax.shard_map(
        local,
        mesh=mesh,
        in_specs=placed,
        out_specs=(P("band", None, "grid", None, None), P("grid", None, None)),
        check_vma=False,
    )
```

profile of v0, /device:TPU:6, one launch (start us, length us, event | category | flops | bytes accessed | tf_op | source)
XLA Modules:
  0.0 574.2 jit_solution(15256407723588242375)
XLA Ops:
  7.2 3.1 fusion.63
  10.3 2.0 fusion.60
  12.3 2.0 fusion.54
  14.3 2.0 fusion.55
  16.3 2.0 fusion.170
  18.2 2.0 fusion.53
  20.2 1.9 copy.242
  22.1 19.1 %all-to-all-start = ((f32[1,3,192,192]{3,0,1,2:T(1,128)}), f32[1,3,192,192]{3,0,1,2:T(1,128)S(1)}, u32[]{:S(2)}, u32[]{:S(2)}) async-start(f32[1,3,192,192]{3,0,1,2:T(1,128)} %copy.242), calls=%async_computation | async-start | bytes 1179648 | tf_op jit(solution)/shard_map/all_to_all | solution.py:49
  41.2 2.0 fusion.166
  43.2 2.0 fusion.52
  46.6 14.3 %all-to-all-done = f32[1,3,192,192]{3,0,1,2:T(1,128)S(1)} async-done(((f32[1,3,192,192]{3,0,1,2:T(1,128)}), f32[1,3,192,192]{3,0,1,2:T(1,128)S(1)}, u32[]{:S(2)}, u32[]{:S(2)}) %all-to-all-start) | async-done | bytes 442400 | tf_op jit(solution)/shard_map/all_to_all | solution.py:49
  60.9 9.6 %all-to-all-start.1 = ((f32[1,3,192,192]{3,0,1,2:T(1,128)}), f32[1,3,192,192]{3,0,1,2:T(1,128)S(1)}, u32[]{:S(2)}, u32[]{:S(2)}) async-start(f32[1,3,192,192]{3,0,1,2:T(1,128)} %copy.250), calls=%async_computation.1 | async-start | bytes 1179648 | tf_op jit(solution)/shard_map/all_to_all | solution.py:48
  71.8 19.9 %all-to-all-done.1 = f32[1,3,192,192]{3,0,1,2:T(1,128)S(1)} async-done(((f32[1,3,192,192]{3,0,1,2:T(1,128)}), f32[1,3,192,192]{3,0,1,2:T(1,128)S(1)}, u32[]{:S(2)}, u32[]{:S(2)}) %all-to-all-start.1) | async-done | bytes 442400 | tf_op jit(solution)/shard_map/all_to_all | solution.py:48
  104.9 8.0 %all-to-all-start.3 = ((f32[1,192,3,192]{3,0,2,1:T(1,128)}), f32[1,192,3,192]{3,0,2,1:T(1,128)S(1)}, u32[]{:S(2)}, u32[]{:S(2)}) async-start(f32[1,192,3,192]{3,0,2,1:T(1,128)} %copy.263), calls=%async_computation.3 | async-start | bytes 1179648 | tf_op jit(solution)/shard_map/all_to_all | solution.py:57
  117.3 16.8 %all-to-all-done.3 = f32[1,192,3,192]{3,0,2,1:T(1,128)S(1)} async-done(((f32[1,192,3,192]{3,0,2,1:T(1,128)}), f32[1,192,3,192]{3,0,2,1:T(1,128)S(1)}, u32[]{:S(2)}, u32[]{:S(2)}) %all-to-all-start.3) | async-done | bytes 442400 | tf_op jit(solution)/shard_map/all_to_all | solution.py:57
  134.1 7.9 %all-to-all-start.2 = ((f32[1,192,3,192]{3,0,2,1:T(1,128)}), f32[1,192,3,192]{3,0,2,1:T(1,128)}, u32[]{:S(2)}, u32[]{:S(2)}) async-start(f32[1,192,3,192]{3,0,2,1:T(1,128)} %copy.258), calls=%async_computation.2 | async-start | bytes 1179648 | tf_op jit(solution)/shard_map/all_to_all | solution.py:58
  143.7 19.3 %all-to-all-done.2 = f32[1,192,3,192]{3,0,2,1:T(1,128)} async-done(((f32[1,192,3,192]{3,0,2,1:T(1,128)}), f32[1,192,3,192]{3,0,2,1:T(1,128)}, u32[]{:S(2)}, u32[]{:S(2)}) %all-to-all-start.2) | async-done | bytes 442400 | tf_op jit(solution)/shard_map/all_to_all | solution.py:58
  163.1 2.1 copy.259
  176.6 1.6 fusion.41
  188.9 8.1 %all-to-all-start.4 = ((f32[1,3,192,192]{3,0,1,2:T(1,128)}), f32[1,3,192,192]{3,0,1,2:T(1,128)}, u32[]{:S(2)}, u32[]{:S(2)}) async-start(f32[1,3,192,192]{3,0,1,2:T(1,128)} %copy.270), calls=%async_computation.4 | async-start | bytes 1179648 | tf_op jit(solution)/shard_map/all_to_all | solution.py:48
  201.3 16.4 %all-to-all-done.4 = f32[1,3,192,192]{3,0,1,2:T(1,128)} async-done(((f32[1,3,192,192]{3,0,1,2:T(1,128)}), f32[1,3,192,192]{3,0,1,2:T(1,128)}, u32[]{:S(2)}, u32[]{:S(2)}) %all-to-all-start.4) | async-done | bytes 442400 | tf_op jit(solution)/shard_map/all_to_all | solution.py:48
  217.8 8.3 %all-to-all-start.5 = ((f32[1,3,192,192]{3,0,1,2:T(1,128)}), f32[1,3,192,192]{3,0,1,2:T(1,128)}, u32[]{:S(2)}, u32[]{:S(2)}) async-start(f32[1,3,192,192]{3,0,1,2:T(1,128)} %copy.276), calls=%async_computation.5 | async-start | bytes 1179648 | tf_op jit(solution)/shard_map/all_to_all | solution.py:49
  230.3 16.8 %all-to-all-done.5 = f32[1,3,192,192]{3,0,1,2:T(1,128)} async-done(((f32[1,3,192,192]{3,0,1,2:T(1,128)}), f32[1,3,192,192]{3,0,1,2:T(1,128)}, u32[]{:S(2)}, u32[]{:S(2)}) %all-to-all-start.5) | async-done | bytes 442400 | tf_op jit(solution)/shard_map/all_to_all | solution.py:49
  249.8 2.2 reshape.437
  252.1 2.5 fusion.131
  256.0 2.6 fusion.34
  264.4 8.0 %all-to-all-start.7 = ((f32[1,192,3,192]{3,0,2,1:T(1,128)}), f32[1,192,3,192]{3,0,2,1:T(1,128)}, u32[]{:S(2)}, u32[]{:S(2)}) async-start(f32[1,192,3,192]{3,0,2,1:T(1,128)} %copy.289), calls=%async_computation.7 | async-start | bytes 1179648 | tf_op jit(solution)/shard_map/all_to_all | solution.py:58
  272.4 2.5 fusion.139
  277.8 15.7 %all-to-all-done.7 = f32[1,192,3,192]{3,0,2,1:T(1,128)} async-done(((f32[1,192,3,192]{3,0,2,1:T(1,128)}), f32[1,192,3,192]{3,0,2,1:T(1,128)}, u32[]{:S(2)}, u32[]{:S(2)}) %all-to-all-start.7) | async-done | bytes 442400 | tf_op jit(solution)/shard_map/all_to_all | solution.py:58
  293.5 7.9 %all-to-all-start.6 = ((f32[1,192,3,192]{3,0,2,1:T(1,128)}), f32[1,192,3,192]{3,0,2,1:T(1,128)}, u32[]{:S(2)}, u32[]{:S(2)}) async-start(f32[1,192,3,192]{3,0,2,1:T(1,128)} %copy.284), calls=%async_computation.6 | async-start | bytes 1179648 | tf_op jit(solution)/shard_map/all_to_all | solution.py:57
  302.2 2.1 copy.290
  305.7 16.7 %all-to-all-done.6 = f32[1,192,3,192]{3,0,2,1:T(1,128)} async-done(((f32[1,192,3,192]{3,0,2,1:T(1,128)}), f32[1,192,3,192]{3,0,2,1:T(1,128)}, u32[]{:S(2)}, u32[]{:S(2)}) %all-to-all-start.6) | async-done | bytes 442400 | tf_op jit(solution)/shard_map/all_to_all | solution.py:57
  322.5 2.1 copy.285
  324.6 2.2 reshape.438
  326.9 2.5 fusion.141
  336.5 1.5 fusion.25
  338.0 3.0 add_multiply_fusion.1
  342.5 69.9 %all-reduce.2.cloned.1.call-done = f32[3,192,192]{2,1,0:T(8,128)} async-done(((f32[3,192,192]{2,1,0:T(8,128)}), f32[3,192,192]{2,1,0:T(8,128)}) %all-reduce.2.cloned.1.call-update) | async-done | bytes 442384 | tf_op jit(solution)/shard_map/psum | solution.py:105
  412.4 2.5 fusion.148
  422.1 14.0 %all-to-all-start.9 = ((f32[1,3,192,192]{3,0,1,2:T(1,128)}), f32[1,3,192,192]{3,0,1,2:T(1,128)}, u32[]{:S(2)}, u32[]{:S(2)}) async-start(f32[1,3,192,192]{3,0,1,2:T(1,128)} %copy.302), calls=%async_computation.9 | async-start | bytes 1179648 | tf_op jit(solution)/shard_map/all_to_all | solution.py:49
  440.3 16.0 %all-to-all-done.9 = f32[1,3,192,192]{3,0,1,2:T(1,128)} async-done(((f32[1,3,192,192]{3,0,1,2:T(1,128)}), f32[1,3,192,192]{3,0,1,2:T(1,128)}, u32[]{:S(2)}, u32[]{:S(2)}) %all-to-all-start.9) | async-done | bytes 442400 | tf_op jit(solution)/shard_map/all_to_all | solution.py:49
  456.3 7.8 %all-to-all-start.8 = ((f32[1,3,192,192]{3,0,1,2:T(1,128)}), f32[1,3,192,192]{3,0,1,2:T(1,128)S(1)}, u32[]{:S(2)}, u32[]{:S(2)}) async-start(f32[1,3,192,192]{3,0,1,2:T(1,128)} %copy.296), calls=%async_computation.8 | async-start | bytes 1179648 | tf_op jit(solution)/shard_map/all_to_all | solution.py:48
  466.4 19.1 %all-to-all-done.8 = f32[1,3,192,192]{3,0,1,2:T(1,128)S(1)} async-done(((f32[1,3,192,192]{3,0,1,2:T(1,128)}), f32[1,3,192,192]{3,0,1,2:T(1,128)S(1)}, u32[]{:S(2)}, u32[]{:S(2)}) %all-to-all-start.8) | async-done | bytes 442400 | tf_op jit(solution)/shard_map/all_to_all | solution.py:48
  496.8 7.8 %all-to-all-start.10 = ((f32[1,192,3,192]{3,0,2,1:T(1,128)}), f32[1,192,3,192]{3,0,2,1:T(1,128)}, u32[]{:S(2)}, u32[]{:S(2)}) async-start(f32[1,192,3,192]{3,0,2,1:T(1,128)} %copy.310), calls=%async_computation.10 | async-start | bytes 1179648 | tf_op jit(solution)/shard_map/all_to_all | solution.py:57
  509.0 16.9 %all-to-all-done.10 = f32[1,192,3,192]{3,0,2,1:T(1,128)} async-done(((f32[1,192,3,192]{3,0,2,1:T(1,128)}), f32[1,192,3,192]{3,0,2,1:T(1,128)}, u32[]{:S(2)}, u32[]{:S(2)}) %all-to-all-start.10) | async-done | bytes 442400 | tf_op jit(solution)/shard_map/all_to_all | solution.py:57
  526.0 7.6 %all-to-all-start.11 = ((f32[1,192,3,192]{3,0,2,1:T(1,128)}), f32[1,192,3,192]{3,0,2,1:T(1,128)S(1)}, u32[]{:S(2)}, u32[]{:S(2)}) async-start(f32[1,192,3,192]{3,0,2,1:T(1,128)} %copy.315), calls=%async_computation.11 | async-start | bytes 1179648 | tf_op jit(solution)/shard_map/all_to_all | solution.py:58
  536.2 18.6 %all-to-all-done.11 = f32[1,192,3,192]{3,0,2,1:T(1,128)S(1)} async-done(((f32[1,192,3,192]{3,0,2,1:T(1,128)}), f32[1,192,3,192]{3,0,2,1:T(1,128)S(1)}, u32[]{:S(2)}, u32[]{:S(2)}) %all-to-all-start.11) | async-done | bytes 442400 | tf_op jit(solution)/shard_map/all_to_all | solution.py:58
  564.4 2.6 fusion.1
  (126 shorter events, 116.3 us)
Async XLA Ops:
  7.2 3.1 copy-start
  22.1 38.8 %all-to-all-start = ((f32[1,3,192,192]{3,0,1,2:T(1,128)}), f32[1,3,192,192]{3,0,1,2:T(1,128)S(1)}, u32[]{:S(2)}, u32[]{:S(2)}) async-start(f32[1,3,192,192]{3,0,1,2:T(1,128)} %copy.242), calls=%async_computation | async-start | bytes 1179648 | tf_op jit(solution)/shard_map/all_to_all | solution.py:49
  60.9 30.8 %all-to-all-start.1 = ((f32[1,3,192,192]{3,0,1,2:T(1,128)}), f32[1,3,192,192]{3,0,1,2:T(1,128)S(1)}, u32[]{:S(2)}, u32[]{:S(2)}) async-start(f32[1,3,192,192]{3,0,1,2:T(1,128)} %copy.250), calls=%async_computation.1 | async-start | bytes 1179648 | tf_op jit(solution)/shard_map/all_to_all | solution.py:48
  104.9 29.2 %all-to-all-start.3 = ((f32[1,192,3,192]{3,0,2,1:T(1,128)}), f32[1,192,3,192]{3,0,2,1:T(1,128)S(1)}, u32[]{:S(2)}, u32[]{:S(2)}) async-start(f32[1,192,3,192]{3,0,2,1:T(1,128)} %copy.263), calls=%async_computation.3 | async-start | bytes 1179648 | tf_op jit(solution)/shard_map/all_to_all | solution.py:57
  115.9 26.2 %copy-start.13 = (f32[3,192,192]{2,1,0:T(8,128)S(1)}, f32[3,192,192]{2,1,0:T(8,128)}, u32[]{:S(2)}) copy-start(f32[3,192,192]{2,1,0:T(8,128)} %param.6) | copy-start | bytes 1327108
  115.9 26.2 %copy-start.14 = (f32[3,192,192]{2,1,0:T(8,128)S(1)}, f32[3,192,192]{2,1,0:T(8,128)}, u32[]{:S(2)}) copy-start(f32[3,192,192]{2,1,0:T(8,128)} %param.7) | copy-start | bytes 1327108
  134.1 8.0 %copy-start.8 = (f32[1,192,3,192]{3,0,2,1:T(1,128)}, f32[1,192,3,192]{3,0,2,1:T(1,128)S(1)}, u32[]{:S(2)}) copy-start(f32[1,192,3,192]{3,0,2,1:T(1,128)S(1)} %all-to-all-done.3) | copy-start | bytes 1327108
  134.1 29.0 %all-to-all-start.2 = ((f32[1,192,3,192]{3,0,2,1:T(1,128)}), f32[1,192,3,192]{3,0,2,1:T(1,128)}, u32[]{:S(2)}, u32[]{:S(2)}) async-start(f32[1,192,3,192]{3,0,2,1:T(1,128)} %copy.258), calls=%async_computation.2 | async-start | bytes 1179648 | tf_op jit(solution)/shard_map/all_to_all | solution.py:58
  183.8 0.8 copy-start.1
  188.9 28.9 %all-to-all-start.4 = ((f32[1,3,192,192]{3,0,1,2:T(1,128)}), f32[1,3,192,192]{3,0,1,2:T(1,128)}, u32[]{:S(2)}, u32[]{:S(2)}) async-start(f32[1,3,192,192]{3,0,1,2:T(1,128)} %copy.270), calls=%async_computation.4 | async-start | bytes 1179648 | tf_op jit(solution)/shard_map/all_to_all | solution.py:48
  197.0 1.4 copy-start.2
  217.8 29.3 %all-to-all-start.5 = ((f32[1,3,192,192]{3,0,1,2:T(1,128)}), f32[1,3,192,192]{3,0,1,2:T(1,128)}, u32[]{:S(2)}, u32[]{:S(2)}) async-start(f32[1,3,192,192]{3,0,1,2:T(1,128)} %copy.276), calls=%async_computation.5 | async-start | bytes 1179648 | tf_op jit(solution)/shard_map/all_to_all | solution.py:49
  230.3 24.3 %copy-start.5 = (f32[192,3,192]{2,0,1:T(8,128)}, f32[192,3,192]{2,0,1:T(8,128)S(1)}, u32[]{:S(2)}) copy-start(f32[192,3,192]{2,0,1:T(8,128)S(1)} %reshape.436) | copy-start | bytes 1327108
  256.0 2.6 copy-start.6
  260.1 1.4 copy-start.3
  264.4 29.1 %all-to-all-start.7 = ((f32[1,192,3,192]{3,0,2,1:T(1,128)}), f32[1,192,3,192]{3,0,2,1:T(1,128)}, u32[]{:S(2)}, u32[]{:S(2)}) async-start(f32[1,192,3,192]{3,0,2,1:T(1,128)} %copy.289), calls=%async_computation.7 | async-start | bytes 1179648 | tf_op jit(solution)/shard_map/all_to_all | solution.py:58
  293.5 29.0 %all-to-all-start.6 = ((f32[1,192,3,192]{3,0,2,1:T(1,128)}), f32[1,192,3,192]{3,0,2,1:T(1,128)}, u32[]{:S(2)}, u32[]{:S(2)}) async-start(f32[1,192,3,192]{3,0,2,1:T(1,128)} %copy.284), calls=%async_computation.6 | async-start | bytes 1179648 | tf_op jit(solution)/shard_map/all_to_all | solution.py:57
  301.5 110.9 %all-reduce.2.cloned.1.call-start = ((), (), s32[]{:S(2)}) async-start(), calls=%async_computation.12 | async-start | bytes 1179648 | tf_op jit(solution)/shard_map/psum | solution.py:105
  330.8 1.5 copy-start.7
  412.4 3.9 copy-start.4
  422.1 34.3 %all-to-all-start.9 = ((f32[1,3,192,192]{3,0,1,2:T(1,128)}), f32[1,3,192,192]{3,0,1,2:T(1,128)}, u32[]{:S(2)}, u32[]{:S(2)}) async-start(f32[1,3,192,192]{3,0,1,2:T(1,128)} %copy.302), calls=%async_computation.9 | async-start | bytes 1179648 | tf_op jit(solution)/shard_map/all_to_all | solution.py:49
  456.3 29.2 %all-to-all-start.8 = ((f32[1,3,192,192]{3,0,1,2:T(1,128)}), f32[1,3,192,192]{3,0,1,2:T(1,128)S(1)}, u32[]{:S(2)}, u32[]{:S(2)}) async-start(f32[1,3,192,192]{3,0,1,2:T(1,128)} %copy.296), calls=%async_computation.8 | async-start | bytes 1179648 | tf_op jit(solution)/shard_map/all_to_all | solution.py:48
  486.7 1.4 copy-start.10
  489.5 1.5 copy-start.11
  496.8 29.1 %all-to-all-start.10 = ((f32[1,192,3,192]{3,0,2,1:T(1,128)}), f32[1,192,3,192]{3,0,2,1:T(1,128)}, u32[]{:S(2)}, u32[]{:S(2)}) async-start(f32[1,192,3,192]{3,0,2,1:T(1,128)} %copy.310), calls=%async_computation.10 | async-start | bytes 1179648 | tf_op jit(solution)/shard_map/all_to_all | solution.py:57
  507.6 26.0 %copy-start.12 = (f32[3,192,192]{2,1,0:T(8,128)S(1)}, f32[3,192,192]{2,1,0:T(8,128)}, u32[]{:S(2)}) copy-start(f32[3,192,192]{2,1,0:T(8,128)} %get-tuple-element.3) | copy-start | bytes 1327108
  526.0 28.9 %all-to-all-start.11 = ((f32[1,192,3,192]{3,0,2,1:T(1,128)}), f32[1,192,3,192]{3,0,2,1:T(1,128)S(1)}, u32[]{:S(2)}, u32[]{:S(2)}) async-start(f32[1,192,3,192]{3,0,2,1:T(1,128)} %copy.315), calls=%async_computation.11 | async-start | bytes 1179648 | tf_op jit(solution)/shard_map/all_to_all | solution.py:58
  554.9 0.8 copy-start.9
Sparse Core Ops, SparseCore 0:
  341.2 71.1 all-reduce.1
where the time goes:
time: 585 us; the launch traced here: 574 us
  waiting for transfers between devices  277 us (47%)
  matrix products  114 us (19%)
  starting transfers between devices  114 us (19%)
  local copies, waits for them, and re-layouts  52.3 us (9%)
  between operations  16 us (3%)
    psum x1, waiting for transfers between devices, local(): density = lax.psum(partial_value, 'band')  69.9 us
    all_to_all x3, waiting for transfers between devices, forward(): lax.all_to_all(real_part, 'grid', split_axis=2, concat_axis=1, tiled=True)  55.5 us
    all_to_all x3, waiting for transfers between devices, backward(): lax.all_to_all(imag_part, 'grid', split_axis=1, concat_axis=2, tiled=True)  53.6 us
    all_to_all x3, waiting for transfers between devices, backward(): lax.all_to_all(real_part, 'grid', split_axis=1, concat_axis=2, tiled=True)  50.5 us
    all_to_all x3, waiting for transfers between devices, forward(): lax.all_to_all(imag_part, 'grid', split_axis=2, concat_axis=1, tiled=True)  47.1 us
    all_to_all x3, starting transfers between devices, forward(): lax.all_to_all(imag_part, 'grid', split_axis=2, concat_axis=1, tiled=True)  41.4 us
    dot_general x18, matrix products, transform(): rc = jnp.einsum(form, real_part, cosine, precision=high)  30.9 us
    dot_general x17, matrix products, transform(): rs = jnp.einsum(form, real_part, sine, precision=high)  28.4 us
  transfers between devices with their start and end apart: 13, of which 13 were waited for; matrix products, arithmetic and copies ran while one was open for 8% of the time, Pallas kernels for 0%

commit v1 on v0

--- a/solution.py
+++ b/solution.py
@@ -8,6 +8,12 @@
 BESSEL_ONE = 0.36884204609417703
 BESSEL_TWO = 0.07581776248
 XC_FACTOR = 0.98474502
+
+
+def exchange_blocks(x, axis, split, join):
+    pieces = jnp.split(x, lax.axis_size(axis), axis=split)
+    arrived = lax.all_to_all(jnp.stack(pieces), axis, 0, 0)
+    return jnp.concatenate(arrived, axis=join)
 
 
 def tables(length):
@@ -55,7 +61,7 @@
     real_part, imag_part = along_x(real_part, imag_part, True)
     real_part, imag_part = (
         lax.all_to_all(real_part, "grid", split_axis=1, concat_axis=2, tiled=True),
-        lax.all_to_all(imag_part, "grid", split_axis=1, concat_axis=2, tiled=True),
+        exchange_blocks(imag_part, "grid", 1, 2),
     )
     real_part, imag_part = along_y(real_part, imag_part, True)
     real_part, imag_part = along_z(real_part, imag_part, True)

time: 585 us -> 579 us (0.990)
  waiting for transfers between devices: 277 us -> 265 us
    all_to_all x3, waiting for transfers between devices: 55.5 us -> 49.4 us  [forward(): lax.all_to_all(real_part, 'grid', split_axis=2, concat_axis=1, tiled=True)]
    another operation x12 -> x18, local copies, waits for them, and re-layouts: 12 us -> 16.3 us
  transfers between devices with their start and end apart: 13 -> 13, of which waited for: 13 -> 13; matrix products, arithmetic and copies ran while one was open for 8% -> 10% of each run, Pallas kernels for 0% -> 0%
where the time goes in v1:
time: 579 us; the launch traced here: 568 us
  waiting for transfers between devices  265 us (46%)
  matrix products  117 us (20%)
  starting transfers between devices  114 us (20%)
  local copies, waits for them, and re-layouts  54.4 us (9%)
  between operations  16.9 us (3%)
    psum x1, waiting for transfers between devices, local(): density = lax.psum(partial_value, 'band')  70.2 us
    all_to_all x3, waiting for transfers between devices, backward(): lax.all_to_all(real_part, 'grid', split_axis=1, concat_axis=2, tiled=True)  50 us
    all_to_all x3, waiting for transfers between devices, forward(): lax.all_to_all(real_part, 'grid', split_axis=2, concat_axis=1, tiled=True)  49.4 us
    all_to_all x3, waiting for transfers between devices, exchange_blocks(): arrived = lax.all_to_all(jnp.stack(pieces), axis, 0, 0)  49.3 us
    all_to_all x3, waiting for transfers between devices, forward(): lax.all_to_all(imag_part, 'grid', split_axis=2, concat_axis=1, tiled=True)  45.8 us
    all_to_all x3, starting transfers between devices, forward(): lax.all_to_all(imag_part, 'grid', split_axis=2, concat_axis=1, tiled=True)  41.2 us
    dot_general x17, matrix products, transform(): rs = jnp.einsum(form, real_part, sine, precision=high)  30.4 us
    dot_general x18, matrix products, transform(): rc = jnp.einsum(form, real_part, cosine, precision=high)  29.8 us
  transfers between devices with their start and end apart: 13, of which 13 were waited for; matrix products, arithmetic and copies ran while one was open for 10% of the time, Pallas kernels for 0%

profile of v1, /device:TPU:6, one launch (start us, length us, event | category | flops | bytes accessed | tf_op | source)
XLA Modules:
  0.0 568.4 jit_solution(5535399090222595006)
XLA Ops:
  7.2 3.1 fusion.60
  10.3 2.0 fusion.63
  12.3 2.0 fusion.55
  14.3 2.0 fusion.170
  16.3 2.0 fusion.54
  18.2 2.0 fusion.53
  22.1 19.1 %all-to-all-start = ((f32[1,3,192,192]{3,0,1,2:T(1,128)}), f32[1,3,192,192]{3,0,1,2:T(1,128)S(1)}, u32[]{:S(2)}, u32[]{:S(2)}) async-start(f32[1,3,192,192]{3,0,1,2:T(1,128)} %copy.331), calls=%async_computation | async-start | bytes 1179648 | tf_op jit(solution)/shard_map/all_to_all | solution.py:55
  41.3 2.0 fusion.166
  43.2 2.0 fusion.52
  46.6 14.3 %all-to-all-done = f32[1,3,192,192]{3,0,1,2:T(1,128)S(1)} async-done(((f32[1,3,192,192]{3,0,1,2:T(1,128)}), f32[1,3,192,192]{3,0,1,2:T(1,128)S(1)}, u32[]{:S(2)}, u32[]{:S(2)}) %all-to-all-start) | async-done | bytes 442400 | tf_op jit(solution)/shard_map/all_to_all | solution.py:55
  60.9 9.7 %all-to-all-start.1 = ((f32[1,3,192,192]{3,0,1,2:T(1,128)}), f32[1,3,192,192]{3,0,1,2:T(1,128)}, u32[]{:S(2)}, u32[]{:S(2)}) async-start(f32[1,3,192,192]{3,0,1,2:T(1,128)} %copy.339), calls=%async_computation.1 | async-start | bytes 1179648 | tf_op jit(solution)/shard_map/all_to_all | solution.py:54
  73.3 18.4 %all-to-all-done.1 = f32[1,3,192,192]{3,0,1,2:T(1,128)} async-done(((f32[1,3,192,192]{3,0,1,2:T(1,128)}), f32[1,3,192,192]{3,0,1,2:T(1,128)}, u32[]{:S(2)}, u32[]{:S(2)}) %all-to-all-start.1) | async-done | bytes 442400 | tf_op jit(solution)/shard_map/all_to_all | solution.py:54
  105.9 7.7 %all-to-all-start.2 = ((f32[64,1,3,3,192]{4,1,3,2,0:T(1,128)}), f32[64,1,3,3,192]{4,1,3,2,0:T(1,128)S(1)}, u32[]{:S(2)}, u32[]{:S(2)}) async-start(f32[64,1,3,3,192]{4,1,3,2,0:T(1,128)} %copy.347), calls=%async_computation.2 | async-start | bytes 1179648 | tf_op jit(solution)/shard_map/all_to_all | solution.py:15
  117.9 16.6 %all-to-all-done.2 = f32[64,1,3,3,192]{4,1,3,2,0:T(1,128)S(1)} async-done(((f32[64,1,3,3,192]{4,1,3,2,0:T(1,128)}), f32[64,1,3,3,192]{4,1,3,2,0:T(1,128)S(1)}, u32[]{:S(2)}, u32[]{:S(2)}) %all-to-all-start.2) | async-done | bytes 442400 | tf_op jit(solution)/shard_map/all_to_all | solution.py:15
  134.5 8.2 %all-to-all-start.3 = ((f32[1,192,3,192]{3,0,2,1:T(1,128)}), f32[1,192,3,192]{3,0,2,1:T(1,128)}, u32[]{:S(2)}, u32[]{:S(2)}) async-start(f32[1,192,3,192]{3,0,2,1:T(1,128)} %copy.352), calls=%async_computation.3 | async-start | bytes 1179648 | tf_op jit(solution)/shard_map/all_to_all | solution.py:63
  145.8 17.5 %all-to-all-done.3 = f32[1,192,3,192]{3,0,2,1:T(1,128)} async-done(((f32[1,192,3,192]{3,0,2,1:T(1,128)}), f32[1,192,3,192]{3,0,2,1:T(1,128)}, u32[]{:S(2)}, u32[]{:S(2)}) %all-to-all-start.3) | async-done | bytes 442400 | tf_op jit(solution)/shard_map/all_to_all | solution.py:63
  163.3 2.1 copy.353
  187.7 8.1 %all-to-all-start.5 = ((f32[1,3,192,192]{3,0,1,2:T(1,128)}), f32[1,3,192,192]{3,0,1,2:T(1,128)}, u32[]{:S(2)}, u32[]{:S(2)}) async-start(f32[1,3,192,192]{3,0,1,2:T(1,128)} %copy.365), calls=%async_computation.5 | async-start | bytes 1179648 | tf_op jit(solution)/shard_map/all_to_all | solution.py:55
  195.8 2.5 fusion.135
  201.2 15.4 %all-to-all-done.5 = f32[1,3,192,192]{3,0,1,2:T(1,128)} async-done(((f32[1,3,192,192]{3,0,1,2:T(1,128)}), f32[1,3,192,192]{3,0,1,2:T(1,128)}, u32[]{:S(2)}, u32[]{:S(2)}) %all-to-all-start.5) | async-done | bytes 442400 | tf_op jit(solution)/shard_map/all_to_all | solution.py:55
  216.6 8.2 %all-to-all-start.4 = ((f32[1,3,192,192]{3,0,1,2:T(1,128)}), f32[1,3,192,192]{3,0,1,2:T(1,128)}, u32[]{:S(2)}, u32[]{:S(2)}) async-start(f32[1,3,192,192]{3,0,1,2:T(1,128)} %copy.359), calls=%async_computation.4 | async-start | bytes 1179648 | tf_op jit(solution)/shard_map/all_to_all | solution.py:54
  229.0 2.3 fusion.131
  231.3 14.3 %all-to-all-done.4 = f32[1,3,192,192]{3,0,1,2:T(1,128)} async-done(((f32[1,3,192,192]{3,0,1,2:T(1,128)}), f32[1,3,192,192]{3,0,1,2:T(1,128)}, u32[]{:S(2)}, u32[]{:S(2)}) %all-to-all-start.4) | async-done | bytes 442400 | tf_op jit(solution)/shard_map/all_to_all | solution.py:54
  252.0 2.6 fusion.34
  261.6 7.9 %all-to-all-start.7 = ((f32[64,1,3,3,192]{4,1,3,2,0:T(1,128)}), f32[64,1,3,3,192]{4,1,3,2,0:T(1,128)}, u32[]{:S(2)}, u32[]{:S(2)}) async-start(f32[64,1,3,3,192]{4,1,3,2,0:T(1,128)} %copy.378), calls=%async_computation.7 | async-start | bytes 1179648 | tf_op jit(solution)/shard_map/all_to_all | solution.py:15
  269.5 2.5 fusion.139
  274.9 15.7 %all-to-all-done.7 = f32[64,1,3,3,192]{4,1,3,2,0:T(1,128)} async-done(((f32[64,1,3,3,192]{4,1,3,2,0:T(1,128)}), f32[64,1,3,3,192]{4,1,3,2,0:T(1,128)}, u32[]{:S(2)}, u32[]{:S(2)}) %all-to-all-start.7) | async-done | bytes 442400 | tf_op jit(solution)/shard_map/all_to_all | solution.py:15
  290.5 8.0 %all-to-all-start.6 = ((f32[1,192,3,192]{3,0,2,1:T(1,128)}), f32[1,192,3,192]{3,0,2,1:T(1,128)}, u32[]{:S(2)}, u32[]{:S(2)}) async-start(f32[1,192,3,192]{3,0,2,1:T(1,128)} %copy.373), calls=%async_computation.6 | async-start | bytes 1179648 | tf_op jit(solution)/shard_map/all_to_all | solution.py:63
  299.2 2.1 copy.379
  302.8 2.3 fusion.127
  305.1 14.3 %all-to-all-done.6 = f32[1,192,3,192]{3,0,2,1:T(1,128)} async-done(((f32[1,192,3,192]{3,0,2,1:T(1,128)}), f32[1,192,3,192]{3,0,2,1:T(1,128)}, u32[]{:S(2)}, u32[]{:S(2)}) %all-to-all-start.6) | async-done | bytes 442400 | tf_op jit(solution)/shard_map/all_to_all | solution.py:63
  319.4 2.1 copy.374
  321.6 2.2 reshape.451
  323.8 2.6 fusion.141
  333.6 3.0 add_multiply_fusion.1
  338.1 70.2 %all-reduce.2.cloned.1.call-done = f32[3,192,192]{2,1,0:T(8,128)} async-done(((f32[3,192,192]{2,1,0:T(8,128)}), f32[3,192,192]{2,1,0:T(8,128)}) %all-reduce.2.cloned.1.call-update) | async-done | bytes 442384 | tf_op jit(solution)/shard_map/psum | solution.py:111
  408.2 2.5 convolution_subtract_fusion.5
  417.9 14.0 %all-to-all-start.9 = ((f32[1,3,192,192]{3,0,1,2:T(1,128)}), f32[1,3,192,192]{3,0,1,2:T(1,128)}, u32[]{:S(2)}, u32[]{:S(2)}) async-start(f32[1,3,192,192]{3,0,1,2:T(1,128)} %copy.391), calls=%async_computation.9 | async-start | bytes 1179648 | tf_op jit(solution)/shard_map/all_to_all | solution.py:55
  436.1 16.0 %all-to-all-done.9 = f32[1,3,192,192]{3,0,1,2:T(1,128)} async-done(((f32[1,3,192,192]{3,0,1,2:T(1,128)}), f32[1,3,192,192]{3,0,1,2:T(1,128)}, u32[]{:S(2)}, u32[]{:S(2)}) %all-to-all-start.9) | async-done | bytes 442400 | tf_op jit(solution)/shard_map/all_to_all | solution.py:55
  452.2 7.7 %all-to-all-start.8 = ((f32[1,3,192,192]{3,0,1,2:T(1,128)}), f32[1,3,192,192]{3,0,1,2:T(1,128)S(1)}, u32[]{:S(2)}, u32[]{:S(2)}) async-start(f32[1,3,192,192]{3,0,1,2:T(1,128)} %copy.385), calls=%async_computation.8 | async-start | bytes 1179648 | tf_op jit(solution)/shard_map/all_to_all | solution.py:54
  462.1 2.3 fusion.115
  464.4 16.8 %all-to-all-done.8 = f32[1,3,192,192]{3,0,1,2:T(1,128)S(1)} async-done(((f32[1,3,192,192]{3,0,1,2:T(1,128)}), f32[1,3,192,192]{3,0,1,2:T(1,128)S(1)}, u32[]{:S(2)}, u32[]{:S(2)}) %all-to-all-start.8) | async-done | bytes 442400 | tf_op jit(solution)/shard_map/all_to_all | solution.py:54
  483.8 2.6 fusion.10
  493.4 7.5 %all-to-all-start.11 = ((f32[64,1,3,3,192]{4,1,3,2,0:T(1,128)}), f32[64,1,3,3,192]{4,1,3,2,0:T(1,128)S(1)}, u32[]{:S(2)}, u32[]{:S(2)}) async-start(f32[64,1,3,3,192]{4,1,3,2,0:T(1,128)} %copy.404), calls=%async_computation.11 | async-start | bytes 1179648 | tf_op jit(solution)/shard_map/all_to_all | solution.py:15
  505.2 17.0 %all-to-all-done.11 = f32[64,1,3,3,192]{4,1,3,2,0:T(1,128)S(1)} async-done(((f32[64,1,3,3,192]{4,1,3,2,0:T(1,128)}), f32[64,1,3,3,192]{4,1,3,2,0:T(1,128)S(1)}, u32[]{:S(2)}, u32[]{:S(2)}) %all-to-all-start.11) | async-done | bytes 442400 | tf_op jit(solution)/shard_map/all_to_all | solution.py:15
  522.2 7.7 %all-to-all-start.10 = ((f32[1,192,3,192]{3,0,2,1:T(1,128)}), f32[1,192,3,192]{3,0,2,1:T(1,128)}, u32[]{:S(2)}, u32[]{:S(2)}) async-start(f32[1,192,3,192]{3,0,2,1:T(1,128)} %copy.399), calls=%async_computation.10 | async-start | bytes 1179648 | tf_op jit(solution)/shard_map/all_to_all | solution.py:63
  533.0 18.2 %all-to-all-done.10 = f32[1,192,3,192]{3,0,2,1:T(1,128)} async-done(((f32[1,192,3,192]{3,0,2,1:T(1,128)}), f32[1,192,3,192]{3,0,2,1:T(1,128)}, u32[]{:S(2)}, u32[]{:S(2)}) %all-to-all-start.10) | async-done | bytes 442400 | tf_op jit(solution)/shard_map/all_to_all | solution.py:63
  558.5 2.6 fusion.1
  (320 shorter events, 119.8 us)
Async XLA Ops:
  7.2 3.1 copy-start
  22.1 38.8 %all-to-all-start = ((f32[1,3,192,192]{3,0,1,2:T(1,128)}), f32[1,3,192,192]{3,0,1,2:T(1,128)S(1)}, u32[]{:S(2)}, u32[]{:S(2)}) async-start(f32[1,3,192,192]{3,0,1,2:T(1,128)} %copy.331), calls=%async_computation | async-start | bytes 1179648 | tf_op jit(solution)/shard_map/all_to_all | solution.py:55
  60.9 30.7 %all-to-all-start.1 = ((f32[1,3,192,192]{3,0,1,2:T(1,128)}), f32[1,3,192,192]{3,0,1,2:T(1,128)}, u32[]{:S(2)}, u32[]{:S(2)}) async-start(f32[1,3,192,192]{3,0,1,2:T(1,128)} %copy.339), calls=%async_computation.1 | async-start | bytes 1179648 | tf_op jit(solution)/shard_map/all_to_all | solution.py:54
  105.9 28.6 %all-to-all-start.2 = ((f32[64,1,3,3,192]{4,1,3,2,0:T(1,128)}), f32[64,1,3,3,192]{4,1,3,2,0:T(1,128)S(1)}, u32[]{:S(2)}, u32[]{:S(2)}) async-start(f32[64,1,3,3,192]{4,1,3,2,0:T(1,128)} %copy.347), calls=%async_computation.2 | async-start | bytes 1179648 | tf_op jit(solution)/shard_map/all_to_all | solution.py:15
  116.4 26.3 %copy-start.14 = (f32[3,192,192]{2,1,0:T(8,128)S(1)}, f32[3,192,192]{2,1,0:T(8,128)}, u32[]{:S(2)}) copy-start(f32[3,192,192]{2,1,0:T(8,128)} %param.6) | copy-start | bytes 1327108
  116.4 26.3 %copy-start.15 = (f32[3,192,192]{2,1,0:T(8,128)S(1)}, f32[3,192,192]{2,1,0:T(8,128)}, u32[]{:S(2)}) copy-start(f32[3,192,192]{2,1,0:T(8,128)} %param.7) | copy-start | bytes 1327108
  134.5 8.4 %copy-start.10 = (f32[64,1,3,3,192]{4,1,3,2,0:T(1,128)}, f32[64,1,3,3,192]{4,1,3,2,0:T(1,128)S(1)}, u32[]{:S(2)}) copy-start(f32[64,1,3,3,192]{4,1,3,2,0:T(1,128)S(1)} %all-to-all-done.2) | copy-start | bytes 1327108
  134.5 28.9 %all-to-all-start.3 = ((f32[1,192,3,192]{3,0,2,1:T(1,128)}), f32[1,192,3,192]{3,0,2,1:T(1,128)}, u32[]{:S(2)}, u32[]{:S(2)}) async-start(f32[1,192,3,192]{3,0,2,1:T(1,128)} %copy.352), calls=%async_computation.3 | async-start | bytes 1179648 | tf_op jit(solution)/shard_map/all_to_all | solution.py:63
  184.0 0.8 copy-start.2
  187.7 28.9 %all-to-all-start.5 = ((f32[1,3,192,192]{3,0,1,2:T(1,128)}), f32[1,3,192,192]{3,0,1,2:T(1,128)}, u32[]{:S(2)}, u32[]{:S(2)}) async-start(f32[1,3,192,192]{3,0,1,2:T(1,128)} %copy.365), calls=%async_computation.5 | async-start | bytes 1179648 | tf_op jit(solution)/shard_map/all_to_all | solution.py:55
  216.6 28.9 %all-to-all-start.4 = ((f32[1,3,192,192]{3,0,1,2:T(1,128)}), f32[1,3,192,192]{3,0,1,2:T(1,128)}, u32[]{:S(2)}, u32[]{:S(2)}) async-start(f32[1,3,192,192]{3,0,1,2:T(1,128)} %copy.359), calls=%async_computation.4 | async-start | bytes 1179648 | tf_op jit(solution)/shard_map/all_to_all | solution.py:54
  229.0 18.0 %copy-start.4 = (f32[192,3,192]{2,0,1:T(8,128)}, f32[192,3,192]{2,0,1:T(8,128)S(1)}, u32[]{:S(2)}) copy-start(f32[192,3,192]{2,0,1:T(8,128)S(1)} %reshape.450) | copy-start | bytes 1327108
  249.7 0.8 copy-start.6
  250.6 1.4 copy-start.8
  252.0 4.0 copy-start.5
  257.5 1.9 copy-start.1
  261.6 28.9 %all-to-all-start.7 = ((f32[64,1,3,3,192]{4,1,3,2,0:T(1,128)}), f32[64,1,3,3,192]{4,1,3,2,0:T(1,128)}, u32[]{:S(2)}, u32[]{:S(2)}) async-start(f32[64,1,3,3,192]{4,1,3,2,0:T(1,128)} %copy.378), calls=%async_computation.7 | async-start | bytes 1179648 | tf_op jit(solution)/shard_map/all_to_all | solution.py:15
  290.5 28.9 %all-to-all-start.6 = ((f32[1,192,3,192]{3,0,2,1:T(1,128)}), f32[1,192,3,192]{3,0,2,1:T(1,128)}, u32[]{:S(2)}, u32[]{:S(2)}) async-start(f32[1,192,3,192]{3,0,2,1:T(1,128)} %copy.373), calls=%async_computation.6 | async-start | bytes 1179648 | tf_op jit(solution)/shard_map/all_to_all | solution.py:63
  298.5 109.7 %all-reduce.2.cloned.1.call-start = ((), (), s32[]{:S(2)}) async-start(), calls=%async_computation.12 | async-start | bytes 1179648 | tf_op jit(solution)/shard_map/psum | solution.py:111
  323.8 2.6 copy-start.7
  323.8 2.6 copy-start.9
  408.2 4.0 copy-start.3
  417.9 34.3 %all-to-all-start.9 = ((f32[1,3,192,192]{3,0,1,2:T(1,128)}), f32[1,3,192,192]{3,0,1,2:T(1,128)}, u32[]{:S(2)}, u32[]{:S(2)}) async-start(f32[1,3,192,192]{3,0,1,2:T(1,128)} %copy.391), calls=%async_computation.9 | async-start | bytes 1179648 | tf_op jit(solution)/shard_map/all_to_all | solution.py:55
  452.2 29.0 %all-to-all-start.8 = ((f32[1,3,192,192]{3,0,1,2:T(1,128)}), f32[1,3,192,192]{3,0,1,2:T(1,128)S(1)}, u32[]{:S(2)}, u32[]{:S(2)}) async-start(f32[1,3,192,192]{3,0,1,2:T(1,128)} %copy.385), calls=%async_computation.8 | async-start | bytes 1179648 | tf_op jit(solution)/shard_map/all_to_all | solution.py:54
  462.1 19.5 %copy-start.11 = (f32[192,3,192]{2,0,1:T(8,128)}, f32[192,3,192]{2,0,1:T(8,128)S(1)}, u32[]{:S(2)}) copy-start(f32[192,3,192]{2,0,1:T(8,128)S(1)} %reshape.457) | copy-start | bytes 1327108
  483.7 4.0 copy-start.12
  493.4 28.8 %all-to-all-start.11 = ((f32[64,1,3,3,192]{4,1,3,2,0:T(1,128)}), f32[64,1,3,3,192]{4,1,3,2,0:T(1,128)S(1)}, u32[]{:S(2)}, u32[]{:S(2)}) async-start(f32[64,1,3,3,192]{4,1,3,2,0:T(1,128)} %copy.404), calls=%async_computation.11 | async-start | bytes 1179648 | tf_op jit(solution)/shard_map/all_to_all | solution.py:15
  503.7 26.2 %copy-start.13 = (f32[3,192,192]{2,1,0:T(8,128)S(1)}, f32[3,192,192]{2,1,0:T(8,128)}, u32[]{:S(2)}) copy-start(f32[3,192,192]{2,1,0:T(8,128)} %get-tuple-element.3) | copy-start | bytes 1327108
  522.2 29.1 %all-to-all-start.10 = ((f32[1,192,3,192]{3,0,2,1:T(1,128)}), f32[1,192,3,192]{3,0,2,1:T(1,128)}, u32[]{:S(2)}, u32[]{:S(2)}) async-start(f32[1,192,3,192]{3,0,2,1:T(1,128)} %copy.399), calls=%async_computation.10 | async-start | bytes 1179648 | tf_op jit(solution)/shard_map/all_to_all | solution.py:63
Sparse Core Ops, SparseCore 0:
  336.8 71.3 all-reduce.1
